TPU v7x, 128 devices: a whole 4x4x4 slice. The times are simulated.
128 devices in a mesh: seq: 32 (over x, z_hi, y), chan: 4 (over z_lo, core).
Axes of the slice: x: 4, y: 4, z: 4 (z_hi: 2, z_lo: 2; z = z_hi * 2 + z_lo), core: 2. Of those that a mesh axis runs over, the one named last changes fastest.
Arguments:
- layer_input: bfloat16 [4096, 16384], P('chan', 'seq'), may hold values from -6 to 6
- query_proj: bfloat16 [4096, 16384], P('chan', 'seq'), may hold values from -6 to 6
- key_proj: bfloat16 [4096, 16384], P('chan', 'seq'), may hold values from -6 to 6
- value_proj: bfloat16 [4096, 16384], P('chan', 'seq'), may hold values from -6 to 6
- filter_taps: float32 [8, 16384], P('chan', 'seq'), may hold values from -1 to 1
- grad_out: bfloat16 [4096, 16384], P('chan', 'seq'), may hold values from -6 to 6
Outputs:
- mixed_out: bfloat16 [4096, 16384], P('chan', 'seq')
- grad_query: bfloat16 [4096, 16384], P('chan', 'seq')
- grad_key: bfloat16 [4096, 16384], P('chan', 'seq')
- grad_value: bfloat16 [4096, 16384], P('chan', 'seq')
- filter_grad: float32 [8, 16384], P('chan', 'seq')
- weight_grad: float32 [4096, 4096], P('seq', 'chan')
All inputs are finite; a program needn't handle non-finite values.
Results may differ from a plain program's by a relative error of at most 0.0058.
Values may be sent and summed in bfloat16 or wider, within the bound.
A program may use at most 128 MiB of HBM per device.

v0:
```python
import math
import jax
import jax.numpy as jnp
from jax import lax
from jax.sharding import PartitionSpec as P

GROUP = 512


def factor_sizes(length):
    padded = 2 * length
    inner_size = math.gcd(length, 2 ** ((padded.bit_length() - 1) // 2))
    return (inner_size, padded // inner_size)


def dft_pair(extent, orient):
    indices = jnp.arange(extent, dtype=jnp.int32)
    phases = indices[:, None] * indices[None, :] % extent
    angles = 2.0 * math.pi / extent * phases.astype(jnp.float32)
    return (jnp.cos(angles), orient * jnp.sin(angles))


def twiddle_pair(outer_size, inner_size, orient):
    total_size = outer_size * inner_size
    outer_index = jnp.arange(outer_size, dtype=jnp.int32)
    inner_index = jnp.arange(inner_size, dtype=jnp.int32)
    phases = outer_index[:, None] * inner_index[None, :] % total_size
    angles = 2.0 * math.pi / total_size * phases.astype(jnp.float32)
    return (jnp.cos(angles), orient * jnp.sin(angles))


def contract(pattern, first_op, second_op):
    return jnp.einsum(
        pattern,
        first_op,
        second_op,
        precision=lax.Precision.HIGHEST,
        preferred_element_type=jnp.float32,
    )


def forward_transform(signal, inner_size, outer_size):
    extent = signal.shape[0]
    blocks = signal.reshape(extent, outer_size // 2, inner_size)
    outer_cos, outer_sin = dft_pair(outer_size, -1.0)
    half_cos = outer_cos[:, : outer_size // 2]
    half_sin = outer_sin[:, : outer_size // 2]
    real_part = contract("kt,pta->pka", half_cos, blocks)
    imag_part = contract("kt,pta->pka", half_sin, blocks)
    twist_cos, twist_sin = twiddle_pair(outer_size, inner_size, -1.0)
    real_twist = real_part * twist_cos - imag_part * twist_sin
    imag_twist = real_part * twist_sin + imag_part * twist_cos
    inner_cos, inner_sin = dft_pair(inner_size, -1.0)
    real_out = contract("pkt,tj->pkj", real_twist, inner_cos) - contract(
        "pkt,tj->pkj", imag_twist, inner_sin
    )
    imag_out = contract("pkt,tj->pkj", real_twist, inner_sin) + contract(
        "pkt,tj->pkj", imag_twist, inner_cos
    )
    return (real_out, imag_out)


def inverse_transform(real_in, imag_in, inner_size, outer_size):
    inner_cos, inner_sin = dft_pair(inner_size, 1.0)
    real_part = contract("pkj,jt->pkt", real_in, inner_cos) - contract(
        "pkj,jt->pkt", imag_in, inner_sin
    )
    imag_part = contract("pkj,jt->pkt", real_in, inner_sin) + contract(
        "pkj,jt->pkt", imag_in, inner_cos
    )
    twist_cos, twist_sin = twiddle_pair(outer_size, inner_size, 1.0)
    real_twist = real_part * twist_cos - imag_part * twist_sin
    imag_twist = real_part * twist_sin + imag_part * twist_cos
    outer_cos, outer_sin = dft_pair(outer_size, 1.0)
    half_cos = outer_cos[: outer_size // 2, :]
    half_sin = outer_sin[: outer_size // 2, :]
    signal = contract("tk,pka->pta", half_cos, real_twist) - contract(
        "tk,pka->pta", half_sin, imag_twist
    )
    extent = real_in.shape[0]
    return signal.reshape(extent, outer_size // 2 * inner_size) * (1.0 / (outer_size * inner_size))


def convolve(input_real, input_imag, taps_real, taps_imag, inner_size, outer_size):
    real_prod = taps_real * input_real - taps_imag * input_imag
    imag_prod = taps_real * input_imag + taps_imag * input_real
    return inverse_transform(real_prod, imag_prod, inner_size, outer_size).astype(jnp.bfloat16)


def correlate(
    up_real, up_imag, input_real, input_imag, taps_real, taps_imag, inner_size, outer_size, factor
):
    real_prod = taps_real * up_real + taps_imag * up_imag
    imag_prod = taps_real * up_imag - taps_imag * up_real
    back_long = inverse_transform(real_prod, imag_prod, inner_size, outer_size).astype(jnp.bfloat16)
    grad_real = jnp.sum(up_real * input_real + up_imag * input_imag, axis=0, keepdims=True)
    grad_imag = jnp.sum(up_imag * input_real - up_real * input_imag, axis=0, keepdims=True)
    taps_grad = inverse_transform(grad_real, grad_imag, inner_size, outer_size) * factor
    return (back_long, taps_grad)


def weight_sum(layer_input, grad_query, factor):
    gathered = lax.all_gather(layer_input, "chan", axis=0, tiled=True)
    summed = lax.psum_scatter(
        jnp.einsum("it,jt->ij", gathered, grad_query, preferred_element_type=jnp.float32),
        "seq",
        scatter_dimension=0,
        tiled=True,
    )
    return summed * factor


def per_device(layer_input, query_proj, key_proj, value_proj, filter_taps, grad_out):
    float_type = jnp.float32
    half_type = jnp.bfloat16
    seq_count = lax.axis_size("seq")
    tok_dev = query_proj.shape[1]
    length = seq_count * tok_dev
    channels = query_proj.shape[0]
    piece_size = channels // seq_count
    inner_size, outer_size = factor_sizes(length)
    weight_factor = 1.0 / math.sqrt(length)
    taps_factor = 1.0 / math.sqrt(GROUP * length)
    mixed_in = (key_proj.astype(float_type) * value_proj.astype(float_type)).astype(half_type)
    upstream = (grad_out.astype(float_type) * query_proj.astype(float_type)).astype(half_type)
    full_taps = lax.all_gather(filter_taps, "seq", axis=1, tiled=True)
    local_group = lax.axis_index("seq") * piece_size // GROUP
    taps_row = lax.dynamic_slice_in_dim(full_taps, local_group, 1, 0)
    taps_real, taps_imag = forward_transform(taps_row, inner_size, outer_size)
    signal = lax.all_to_all(mixed_in, "seq", split_axis=0, concat_axis=1, tiled=True)
    input_real, input_imag = forward_transform(signal.astype(float_type), inner_size, outer_size)
    conv_long = convolve(input_real, input_imag, taps_real, taps_imag, inner_size, outer_size)
    conv_out = lax.all_to_all(conv_long, "seq", split_axis=1, concat_axis=0, tiled=True)
    grad_query = (grad_out.astype(float_type) * conv_out.astype(float_type)).astype(half_type)
    back_signal = lax.all_to_all(upstream, "seq", split_axis=0, concat_axis=1, tiled=True)
    up_real, up_imag = forward_transform(back_signal.astype(float_type), inner_size, outer_size)
    back_long, taps_grad = correlate(
        up_real,
        up_imag,
        input_real,
        input_imag,
        taps_real,
        taps_imag,
        inner_size,
        outer_size,
        taps_factor,
    )
    grad_mixed = lax.all_to_all(back_long, "seq", split_axis=1, concat_axis=0, tiled=True)
    conv_float = conv_out.astype(float_type)
    grad_float = grad_mixed.astype(float_type)
    mixed_out = (query_proj.astype(float_type) * conv_float).astype(half_type)
    grad_key = (grad_float * value_proj.astype(float_type)).astype(half_type)
    grad_value = (grad_float * key_proj.astype(float_type)).astype(half_type)
    selector = (jnp.arange(filter_taps.shape[0], dtype=jnp.int32) == local_group).astype(float_type)
    filter_grad = lax.psum_scatter(
        selector[:, None] * taps_grad, "seq", scatter_dimension=1, tiled=True
    )
    weight_grad = weight_sum(layer_input, grad_query, weight_factor)
    return (mixed_out, grad_query, grad_key, grad_value, filter_grad, weight_grad)


def solution(mesh):
    placed = (
        P("chan", "seq"),
        P("chan", "seq"),
        P("chan", "seq"),
        P("chan", "seq"),
        P("chan", "seq"),
        P("chan", "seq"),
    )
    return jax.shard_map(
        per_device,
        mesh=mesh,
        in_specs=placed,
        out_specs=(
            P("chan", "seq"),
            P("chan", "seq"),
            P("chan", "seq"),
            P("chan", "seq"),
            P("chan", "seq"),
            P("seq", "chan"),
        ),
        check_vma=False,
    )
```

profile of v0, /device:TPU:0, one launch (start us, length us, event | category | flops | bytes accessed | tf_op | source)
XLA Modules:
  0.0 755.0 jit_solution(1742604908414005586)
XLA Ops:
  8.0 2.8 fusion.25
  10.8 10.7 %all-to-all-start.2 = ((bf16[32,32,512]{2,1,0:T(8,128)(2,1)}), bf16[32,32,512]{2,1,0:T(8,128)(2,1)S(1)}, u32[]{:S(2)}, u32[]{:S(2)}) async-start(bf16[32,32,512]{2,1,0:T(8,128)(2,1)} %bitcast.24), calls=%async_computation.2 | async-start | bytes 2097152 | tf_op jit(solution)/shard_map/all_to_all | solution.py:135
  25.0 95.5 %all_gather.6 = f32[2,16384]{1,0:T(2,128)S(1)} all-gather(f32[2,512]{1,0:T(2,128)S(1)} %copy-done.13), channel_id=1, replica_groups=mesh['seq'=32,'chan'=4] {'seq'}, dimensions={1}, use_global_device_ids=true | all-gather | bytes 135168 | tf_op jit(solution)/shard_map/all_gather | solution.py:126
  131.4 7.3 fusion.56
  138.7 7.3 fusion.58
  145.9 7.4 convolution_add_fusion.1
  153.4 7.3 convolution_subtract_fusion.1
  160.7 5.3 fusion.47
  166.0 4.9 fusion.46
  171.0 4.9 convolution_subtract_fusion
  175.9 5.1 convolution_add_fusion
  181.1 3.6 fusion.4
  184.7 3.6 fusion.41
  190.3 18.0 %all_to_all.52 = bf16[32,32,512]{2,0,1:T(8,128)(2,1)S(1)} all-to-all(bf16[32,32,512]{2,0,1:T(8,128)(2,1)S(1)} %copy.120), channel_id=1, replica_groups=mesh['seq'=32,'chan'=4] {'seq'}, dimensions={1} | all-to-all | bytes 2097152 | tf_op jit(solution)/shard_map/all_to_all | solution.py:148
  211.1 8.6 %all-to-all-start = ((bf16[32,32,512]{2,1,0:T(8,128)(2,1)}), bf16[32,32,512]{2,1,0:T(8,128)(2,1)S(1)}, u32[]{:S(2)}, u32[]{:S(2)}) async-start(bf16[32,32,512]{2,1,0:T(8,128)(2,1)} %bitcast.9), calls=%async_computation | async-start | bytes 2097152 | tf_op jit(solution)/shard_map/all_to_all | solution.py:130
  220.5 13.4 %all-to-all-done = bf16[32,32,512]{2,1,0:T(8,128)(2,1)S(1)} async-done(((bf16[32,32,512]{2,1,0:T(8,128)(2,1)}), bf16[32,32,512]{2,1,0:T(8,128)(2,1)S(1)}, u32[]{:S(2)}, u32[]{:S(2)}) %all-to-all-start) | async-done | bytes 1048608 | tf_op jit(solution)/shard_map/all_to_all | solution.py:130
  238.9 9.2 %fusion.50 = f32[32,256,128]{2,1,0:T(8,128)} fusion(f32[32,128,256]{2,1,0:T(8,128)S(1)} %fusion.80, f32[32,128,256]{2,1,0:T(8,128)S(1)} %fusion.84, f32[256,128]{0,1:T(8,128)S(1)} %copy.96, f32[256,128]{0,1:T(8,128)S(1)} %copy.94), kind=kOutput, calls=%fused_computation.71 | convolution fusion | flops 1614004224 | bytes 12845056 | tf_op jit(solution)/shard_map/pkt,tj->pkj/dot_general | solution.py:33
  248.1 7.1 fusion.52
  255.2 7.9 %convolution_subtract_fusion.3 = f32[32,256,128]{2,1,0:T(8,128)S(1)} fusion(f32[32,256,128]{2,1,0:T(8,128)S(1)} %fusion.52, f32[32,128,256]{2,1,0:T(8,128)S(1)} %fusion.80, f32[32,128,256]{2,1,0:T(8,128)S(1)} %fusion.84, f32[256,128]{0,1:T(8,128)S(1)} %copy.96, f32[256,128]{0,1:T(8,128)S(1)} %copy.94), kind=kOutput, calls=%fused_computation.48 | convolution fusion | flops 1615052800 | bytes 17039360 | tf_op jit(solution)/shard_map/pkt,tj->pkj/dot_general | solution.py:33
  263.1 11.4 %subtract_reduce_fusion = (f32[256,128]{1,0:T(8,128)S(1)}, f32[256,128]{1,0:T(8,128)}, f32[32,256,128]{2,1,0:T(8,128)S(1)}) fusion(f32[32,256,128]{2,1,0:T(8,128)S(1)} %copy-done.3, f32[32,256,128]{2,1,0:T(8,128)S(1)} %copy-done.1, f32[32,256,128]{2,1,0:T(8,128)S(1)} %convolution_subtract_fusion.3, f32[32,256,128]{2,1,0:T(8,128)} %fusion.50, ...), kind=kOutput, calls=%fused_computation.13 | convolution fusion | flops 1623359488 | bytes 29884416 | tf_op jit(solution)/shard_map/pkt,tj->pkj/dot_general | solution.py:33
  274.6 4.9 fusion.45
  279.5 4.9 fusion.44
  284.4 5.4 convolution_subtract_fusion.2
  289.8 4.9 convolution_add_fusion.2
  294.8 3.6 fusion.12
  298.4 3.8 fusion.38
  305.2 4.1 all-to-all-start.1
  313.4 5.0 copy.143
  318.5 5.0 all-to-all-done.1
  325.3 12.8 %convolution_bitcast_fusion = f32[4096,1024]{0,1:T(8,128)} fusion(bf16[1024,512]{1,0:T(8,128)(2,1)} %get-tuple-element.35, bf16[4096,512]{1,0:T(8,128)(2,1)} %all-gather.2.cloned.1.call-done), kind=kOutput, calls=%fused_computation | convolution fusion | flops 4294967296 | bytes 22020096 | tf_op jit(solution)/shard_map/it,jt->ij/dot_general | solution.py:105
  338.1 185.3 %reduce-scatter.7.cloned.1.call-done = f32[512,2]{1,0:T(8,128)} async-done(((f32[16384,2]{1,0:T(8,128)}), f32[512,2]{1,0:T(8,128)}) %reduce-scatter.7.cloned.1.call-update) | async-done | bytes 4112
  525.1 220.3 %reduce-scatter.5.cloned.1.call-done = f32[128,1024]{0,1:T(8,128)} async-done(((f32[4096,1024]{0,1:T(8,128)}), f32[128,1024]{0,1:T(8,128)}) %reduce-scatter.5.cloned.1.call-update) | async-done | bytes 524304 | tf_op jit(solution)/shard_map/reduce_scatter | solution.py:104
  (79 shorter events, 37.2 us)
Async XLA Ops:
  8.0 17.0 %copy-start.13 = (f32[2,512]{1,0:T(2,128)S(1)}, f32[2,512]{1,0:T(2,128)}, u32[]{:S(2)}) copy-start(f32[2,512]{1,0:T(2,128)} %param.10) | copy-start | bytes 12292
  10.8 115.1 %all-to-all-start.2 = ((bf16[32,32,512]{2,1,0:T(8,128)(2,1)}), bf16[32,32,512]{2,1,0:T(8,128)(2,1)S(1)}, u32[]{:S(2)}, u32[]{:S(2)}) async-start(bf16[32,32,512]{2,1,0:T(8,128)(2,1)} %bitcast.24), calls=%async_computation.2 | async-start | bytes 2097152 | tf_op jit(solution)/shard_map/all_to_all | solution.py:135
  23.5 211.7 %copy-start.7 = (f32[256,256]{1,0:T(8,128)}, f32[256,256]{1,0:T(8,128)S(1)}, u32[]{:S(2)}) copy-start(f32[256,256]{1,0:T(8,128)S(1)} %fusion.104) | copy-start | bytes 786436
  153.4 22.5 %copy-start = (f32[32,256,128]{2,1,0:T(8,128)}, f32[32,256,128]{2,1,0:T(8,128)S(1)}, u32[]{:S(2)}) copy-start(f32[32,256,128]{2,1,0:T(8,128)S(1)} %convolution_add_fusion.1) | copy-start | bytes 12582916
  160.7 15.2 %copy-start.2 = (f32[32,256,128]{2,1,0:T(8,128)}, f32[32,256,128]{2,1,0:T(8,128)S(1)}, u32[]{:S(2)}) copy-start(f32[32,256,128]{2,1,0:T(8,128)S(1)} %convolution_subtract_fusion.1) | copy-start | bytes 12582916
  189.7 18.6 %copy-start.10 = (bf16[1024,512]{1,0:T(8,128)(2,1)S(1)}, bf16[1024,512]{1,0:T(8,128)(2,1)}, u32[]{:S(2)}) copy-start(bf16[1024,512]{1,0:T(8,128)(2,1)} %param.8) | copy-start | bytes 3145732
  189.7 18.6 %copy-start.11 = (bf16[1024,512]{1,0:T(8,128)(2,1)S(1)}, bf16[1024,512]{1,0:T(8,128)(2,1)}, u32[]{:S(2)}) copy-start(bf16[1024,512]{1,0:T(8,128)(2,1)} %param.9) | copy-start | bytes 3145732
  211.1 22.8 %all-to-all-start = ((bf16[32,32,512]{2,1,0:T(8,128)(2,1)}), bf16[32,32,512]{2,1,0:T(8,128)(2,1)S(1)}, u32[]{:S(2)}, u32[]{:S(2)}) async-start(bf16[32,32,512]{2,1,0:T(8,128)(2,1)} %bitcast.9), calls=%async_computation | async-start | bytes 2097152 | tf_op jit(solution)/shard_map/all_to_all | solution.py:130
  219.7 105.6 %all-gather.2.cloned.1.call-start = ((), (), s32[]{:S(2)}) async-start(), calls=%async_computation.6 | async-start | bytes 5242880 | tf_op jit(solution)/shard_map/all_gather | solution.py:103
  238.9 16.3 %copy-start.4 = (f32[32,128,256]{2,1,0:T(8,128)}, f32[32,128,256]{2,1,0:T(8,128)S(1)}, u32[]{:S(2)}) copy-start(f32[32,128,256]{2,1,0:T(8,128)S(1)} %fusion.80) | copy-start | bytes 12582916
  255.2 7.9 %copy-start.1 = (f32[32,256,128]{2,1,0:T(8,128)S(1)}, f32[32,256,128]{2,1,0:T(8,128)}, u32[]{:S(2)}) copy-start(f32[32,256,128]{2,1,0:T(8,128)} %copy-done) | copy-start | bytes 12582916
  255.2 7.9 %copy-start.3 = (f32[32,256,128]{2,1,0:T(8,128)S(1)}, f32[32,256,128]{2,1,0:T(8,128)}, u32[]{:S(2)}) copy-start(f32[32,256,128]{2,1,0:T(8,128)} %copy-done.2) | copy-start | bytes 12582916
  294.7 3.7 copy-start.8
  302.9 6.4 copy-start.12
  302.9 8.4 %copy-start.9 = (f32[256,256]{1,0:T(8,128)S(1)}, f32[256,256]{1,0:T(8,128)}, u32[]{:S(2)}) copy-start(f32[256,256]{1,0:T(8,128)} %copy-done.7) | copy-start | bytes 786436
  305.2 18.3 %all-to-all-start.1 = ((bf16[32,32,512]{2,0,1:T(8,128)(2,1)}), bf16[32,32,512]{2,0,1:T(8,128)(2,1)S(1)}, u32[]{:S(2)}, u32[]{:S(2)}) async-start(bf16[32,32,512]{2,0,1:T(8,128)(2,1)} %copy.107), calls=%async_computation.1 | async-start | bytes 2097152 | tf_op jit(solution)/shard_map/all_to_all | solution.py:133
  309.2 214.2 %reduce-scatter.7.cloned.1.call-start = ((), (), s32[]{:S(2)}) async-start(), calls=%async_computation.8 | async-start | bytes 8650752
  318.4 5.1 copy-start.5
  318.4 5.1 copy-start.6
  318.4 426.9 %reduce-scatter.5.cloned.1.call-start = ((), (), s32[]{:S(2)}) async-start(), calls=%async_computation.7 | async-start | bytes 17301504 | tf_op jit(solution)/shard_map/reduce_scatter | solution.py:104
Sparse Core Ops, SparseCore 0:
  222.2 47.6 all-gather.1
Sparse Core Ops, SparseCore 1:
  318.5 204.9 reduce-scatter.6
  525.7 219.6 reduce-scatter.4
where the time goes:
time: 763 us; the launch traced here: 755 us
  waiting for transfers between devices  425 us (56%)
  matrix products  149 us (20%)
  blocking collectives  114 us (15%)
  starting transfers between devices  23.5 us (3%)
  between operations  16.3 us (2%)
  local copies, waits for them, and re-layouts  15.9 us (2%)
  other arithmetic  12 us (2%)
    reduce_scatter x1, waiting for transfers between devices, weight_sum(): lax.psum_scatter(jnp.einsum('it,jt->ij', gathered, grad_query, preferred_...  220 us
    unnamed x4, waiting for transfers between devices  186 us
    dot_general x36, matrix products, contract(): jnp.einsum(pattern, first_op, second_op, precision=lax.Precision.HIGHEST,...  136 us
    all_gather x1, blocking collectives, per_device(): full_taps = lax.all_gather(filter_taps, 'seq', axis=1, tiled=True)  95.5 us
    all_to_all x1, blocking collectives, per_device(): lax.all_to_all(back_long, 'seq', split_axis=1, concat_axis=0, tiled=True)  18 us
  transfers between devices with their start and end apart: 6, of which 4 were waited for; matrix products, arithmetic and copies ran while one was open for 14% of the time, Pallas kernels for 0%

commit v1 on v0

--- a/solution.py
+++ b/solution.py
@@ -123,7 +123,9 @@
     taps_factor = 1.0 / math.sqrt(GROUP * length)
     mixed_in = (key_proj.astype(float_type) * value_proj.astype(float_type)).astype(half_type)
     upstream = (grad_out.astype(float_type) * query_proj.astype(float_type)).astype(half_type)
-    full_taps = lax.all_gather(filter_taps, "seq", axis=1, tiled=True)
+    full_taps = jnp.concatenate(
+        lax.all_to_all(jnp.stack([filter_taps] * lax.axis_size("seq")), "seq", 0, 0), axis=1
+    )
     local_group = lax.axis_index("seq") * piece_size // GROUP
     taps_row = lax.dynamic_slice_in_dim(full_taps, local_group, 1, 0)
     taps_real, taps_imag = forward_transform(taps_row, inner_size, outer_size)

time: 763 us -> 695 us (0.911)
  blocking collectives: 114 us -> 22.2 us
  waiting for transfers between devices: 425 us -> 444 us
    all_gather x1 -> x0, blocking collectives: 95.5 us -> none  [per_device(): full_taps = lax.all_gather(filter_taps, 'seq', axis=1, tiled=True)]
    all_to_all x1, waiting for transfers between devices: 0.01 us -> 12.4 us  [per_device(): lax.all_to_all(upstream, 'seq', split_axis=0, concat_axis=1, tiled=True)]
    all_to_all x0 -> x1, starting transfers between devices: none -> 10.7 us  [per_device(): lax.all_to_all(jnp.stack([filter_taps] * lax.axis_size('seq')), 'seq', 0, 0)]
  transfers between devices with their start and end apart: 6 -> 7, of which waited for: 4 -> 6; matrix products, arithmetic and copies ran while one was open for 14% -> 16% of each run, Pallas kernels for 0% -> 0%
where the time goes in v1:
time: 695 us; the launch traced here: 687 us
  waiting for transfers between devices  444 us (64%)
  matrix products  149 us (21%)
  starting transfers between devices  26.2 us (4%)
  blocking collectives  22.2 us (3%)
  local copies, waits for them, and re-layouts  17.3 us (2%)
  between operations  16.3 us (2%)
  other arithmetic  12 us (2%)
    reduce_scatter x1, waiting for transfers between devices, weight_sum(): lax.psum_scatter(jnp.einsum('it,jt->ij', gathered, grad_query, preferred_...  221 us
    unnamed x4, waiting for transfers between devices  181 us
    dot_general x36, matrix products, contract(): jnp.einsum(pattern, first_op, second_op, precision=lax.Precision.HIGHEST,...  136 us
    all_to_all x1, blocking collectives, per_device(): lax.all_to_all(back_long, 'seq', split_axis=1, concat_axis=0, tiled=True)  22.2 us
    all_to_all x1, waiting for transfers between devices, per_device(): lax.all_to_all(mixed_in, 'seq', split_axis=0, concat_axis=1, tiled=True)  17 us
  transfers between devices with their start and end apart: 7, of which 6 were waited for; matrix products, arithmetic and copies ran while one was open for 16% of the time, Pallas kernels for 0%

profile of v1, /device:TPU:0, one launch (start us, length us, event | category | flops | bytes accessed | tf_op | source)
XLA Modules:
  0.0 686.9 jit_solution(4549771737224041437)
XLA Ops:
  9.4 10.7 %all-to-all-start = ((f32[32,2,512]{2,1,0:T(2,128)}), f32[32,2,512]{2,1,0:T(2,128)S(1)}, u32[]{:S(2)}, u32[]{:S(2)}) async-start(f32[32,2,512]{2,1,0:T(2,128)} %stack.2), calls=%async_computation | async-start | bytes 262144 | tf_op jit(solution)/shard_map/all_to_all | solution.py:127
  26.7 3.7 all-to-all-done
  30.3 6.2 all-to-all-start.3
  41.6 12.4 %all-to-all-done.3 = bf16[32,32,512]{2,1,0:T(8,128)(2,1)S(1)} async-done(((bf16[32,32,512]{2,1,0:T(8,128)(2,1)}), bf16[32,32,512]{2,1,0:T(8,128)(2,1)S(1)}, u32[]{:S(2)}, u32[]{:S(2)}) %all-to-all-start.3) | async-done | bytes 1048608 | tf_op jit(solution)/shard_map/all_to_all | solution.py:137
  59.4 7.3 %fusion.56 = f32[32,256,128]{2,1,0:T(8,128)S(1)} fusion(f32[32,128,256]{2,1,0:T(8,128)S(1)} %fusion.78, f32[32,128,256]{2,1,0:T(8,128)S(1)} %fusion.82, f32[256,128]{0,1:T(8,128)S(1)} %copy.96, f32[256,128]{0,1:T(8,128)S(1)} %copy.94), kind=kOutput, calls=%fused_computation.73 | convolution fusion | flops 1614004224 | bytes 12845056 | tf_op jit(solution)/shard_map/pkt,tj->pkj/dot_general | solution.py:33
  66.7 7.3 %fusion.58 = f32[32,256,128]{2,1,0:T(8,128)S(1)} fusion(f32[32,128,256]{2,1,0:T(8,128)S(1)} %fusion.78, f32[32,128,256]{2,1,0:T(8,128)S(1)} %fusion.82, f32[256,128]{0,1:T(8,128)S(1)} %copy.96, f32[256,128]{0,1:T(8,128)S(1)} %copy.94), kind=kOutput, calls=%fused_computation.74 | convolution fusion | flops 1613987840 | bytes 12845056 | tf_op jit(solution)/shard_map/pkt,tj->pkj/dot_general | solution.py:33
  74.0 7.4 %convolution_add_fusion.1 = f32[32,256,128]{2,1,0:T(8,128)S(1)} fusion(f32[32,256,128]{2,1,0:T(8,128)S(1)} %fusion.56, f32[32,128,256]{2,1,0:T(8,128)S(1)} %fusion.78, f32[32,128,256]{2,1,0:T(8,128)S(1)} %fusion.82, f32[256,128]{0,1:T(8,128)S(1)} %copy.96, f32[256,128]{0,1:T(8,128)S(1)} %copy.94), kind=kOutput, calls=%fused_computation.43 | convolution fusion | flops 1615036416 | bytes 17039360 | tf_op jit(solution)/shard_map/pkt,tj->pkj/dot_general | solution.py:33
  81.4 7.3 %convolution_subtract_fusion.1 = f32[32,256,128]{2,1,0:T(8,128)S(1)} fusion(f32[32,256,128]{2,1,0:T(8,128)S(1)} %fusion.58, f32[32,128,256]{2,1,0:T(8,128)S(1)} %fusion.78, f32[32,128,256]{2,1,0:T(8,128)S(1)} %fusion.82, f32[256,128]{0,1:T(8,128)S(1)} %copy.96, f32[256,128]{0,1:T(8,128)S(1)} %copy.94), kind=kOutput, calls=%fused_computation.44 | convolution fusion | flops 1615052800 | bytes 17039360 | tf_op jit(solution)/shard_map/pkt,tj->pkj/dot_general | solution.py:33
  88.8 5.3 fusion.47
  94.1 4.9 fusion.46
  99.0 4.9 convolution_subtract_fusion
  104.0 5.1 convolution_add_fusion
  109.1 3.6 fusion.4
  118.4 22.2 %all_to_all.57 = bf16[32,32,512]{2,0,1:T(8,128)(2,1)S(1)} all-to-all(bf16[32,32,512]{2,0,1:T(8,128)(2,1)S(1)} %copy.120), channel_id=1, replica_groups=mesh['seq'=32,'chan'=4] {'seq'}, dimensions={1} | all-to-all | bytes 2097152 | tf_op jit(solution)/shard_map/all_to_all | solution.py:150
  143.3 4.6 all-to-all-start.1
  148.7 17.0 %all-to-all-done.1 = bf16[32,32,512]{2,1,0:T(8,128)(2,1)S(1)} async-done(((bf16[32,32,512]{2,1,0:T(8,128)(2,1)}), bf16[32,32,512]{2,1,0:T(8,128)(2,1)S(1)}, u32[]{:S(2)}, u32[]{:S(2)}) %all-to-all-start.1) | async-done | bytes 1048608 | tf_op jit(solution)/shard_map/all_to_all | solution.py:132
  170.7 9.1 %fusion.50 = f32[32,256,128]{2,1,0:T(8,128)} fusion(f32[32,128,256]{2,1,0:T(8,128)S(1)} %fusion.80, f32[32,128,256]{2,1,0:T(8,128)S(1)} %fusion.84, f32[256,128]{0,1:T(8,128)S(1)} %copy.96, f32[256,128]{0,1:T(8,128)S(1)} %copy.94), kind=kOutput, calls=%fused_computation.71 | convolution fusion | flops 1614004224 | bytes 12845056 | tf_op jit(solution)/shard_map/pkt,tj->pkj/dot_general | solution.py:33
  179.8 7.1 %fusion.52 = f32[32,256,128]{2,1,0:T(8,128)S(1)} fusion(f32[32,128,256]{2,1,0:T(8,128)S(1)} %fusion.80, f32[32,128,256]{2,1,0:T(8,128)S(1)} %fusion.84, f32[256,128]{0,1:T(8,128)S(1)} %copy.96, f32[256,128]{0,1:T(8,128)S(1)} %copy.94), kind=kOutput, calls=%fused_computation.72 | convolution fusion | flops 1613987840 | bytes 12845056 | tf_op jit(solution)/shard_map/pkt,tj->pkj/dot_general | solution.py:33
  187.0 7.9 %convolution_subtract_fusion.3 = f32[32,256,128]{2,1,0:T(8,128)S(1)} fusion(f32[32,256,128]{2,1,0:T(8,128)S(1)} %fusion.52, f32[32,128,256]{2,1,0:T(8,128)S(1)} %fusion.80, f32[32,128,256]{2,1,0:T(8,128)S(1)} %fusion.84, f32[256,128]{0,1:T(8,128)S(1)} %copy.96, f32[256,128]{0,1:T(8,128)S(1)} %copy.94), kind=kOutput, calls=%fused_computation.48 | convolution fusion | flops 1615052800 | bytes 17039360 | tf_op jit(solution)/shard_map/pkt,tj->pkj/dot_general | solution.py:33
  194.9 11.4 %subtract_reduce_fusion = (f32[256,128]{1,0:T(8,128)S(1)}, f32[256,128]{1,0:T(8,128)}, f32[32,256,128]{2,1,0:T(8,128)S(1)}) fusion(f32[32,256,128]{2,1,0:T(8,128)S(1)} %copy-done.3, f32[32,256,128]{2,1,0:T(8,128)S(1)} %copy-done.1, f32[32,256,128]{2,1,0:T(8,128)S(1)} %convolution_subtract_fusion.3, f32[32,256,128]{2,1,0:T(8,128)} %fusion.50, ...), kind=kOutput, calls=%fused_computation.13 | convolution fusion | flops 1623359488 | bytes 29884416 | tf_op jit(solution)/shard_map/pkt,tj->pkj/dot_general | solution.py:33
  206.3 4.9 fusion.45
  211.2 4.9 fusion.44
  216.1 5.4 convolution_subtract_fusion.2
  221.5 4.9 convolution_add_fusion.2
  226.5 3.6 fusion.12
  230.1 3.8 fusion.38
  236.9 4.6 all-to-all-start.2
  245.6 5.0 copy.143
  250.7 8.4 %all-to-all-done.2 = bf16[32,32,512]{2,0,1:T(8,128)(2,1)S(1)} async-done(((bf16[32,32,512]{2,0,1:T(8,128)(2,1)}), bf16[32,32,512]{2,0,1:T(8,128)(2,1)S(1)}, u32[]{:S(2)}, u32[]{:S(2)}) %all-to-all-start.2) | async-done | bytes 1048608 | tf_op jit(solution)/shard_map/all_to_all | solution.py:135
  261.0 12.8 %convolution_bitcast_fusion = f32[4096,1024]{0,1:T(8,128)} fusion(bf16[1024,512]{1,0:T(8,128)(2,1)} %get-tuple-element.35, bf16[4096,512]{1,0:T(8,128)(2,1)} %all-gather.2.cloned.1.call-done), kind=kOutput, calls=%fused_computation | convolution fusion | flops 4294967296 | bytes 22020096 | tf_op jit(solution)/shard_map/it,jt->ij/dot_general | solution.py:105
  273.8 180.5 %reduce-scatter.7.cloned.1.call-done = f32[512,2]{1,0:T(8,128)} async-done(((f32[16384,2]{1,0:T(8,128)}), f32[512,2]{1,0:T(8,128)}) %reduce-scatter.7.cloned.1.call-update) | async-done | bytes 4112
  456.0 221.2 %reduce-scatter.5.cloned.1.call-done = f32[128,1024]{0,1:T(8,128)} async-done(((f32[4096,1024]{0,1:T(8,128)}), f32[128,1024]{0,1:T(8,128)}) %reduce-scatter.5.cloned.1.call-update) | async-done | bytes 524304 | tf_op jit(solution)/shard_map/reduce_scatter | solution.py:104
  (79 shorter events, 45.0 us)
Async XLA Ops:
  9.4 21.0 %all-to-all-start = ((f32[32,2,512]{2,1,0:T(2,128)}), f32[32,2,512]{2,1,0:T(2,128)S(1)}, u32[]{:S(2)}, u32[]{:S(2)}) async-start(f32[32,2,512]{2,1,0:T(2,128)} %stack.2), calls=%async_computation | async-start | bytes 262144 | tf_op jit(solution)/shard_map/all_to_all | solution.py:127
  26.7 140.3 %copy-start.7 = (f32[256,256]{1,0:T(8,128)}, f32[256,256]{1,0:T(8,128)S(1)}, u32[]{:S(2)}) copy-start(f32[256,256]{1,0:T(8,128)S(1)} %fusion.104) | copy-start | bytes 786436
  30.3 23.7 %all-to-all-start.3 = ((bf16[32,32,512]{2,1,0:T(8,128)(2,1)}), bf16[32,32,512]{2,1,0:T(8,128)(2,1)S(1)}, u32[]{:S(2)}, u32[]{:S(2)}) async-start(bf16[32,32,512]{2,1,0:T(8,128)(2,1)} %bitcast.26), calls=%async_computation.3 | async-start | bytes 2097152 | tf_op jit(solution)/shard_map/all_to_all | solution.py:137
  81.4 22.5 %copy-start = (f32[32,256,128]{2,1,0:T(8,128)}, f32[32,256,128]{2,1,0:T(8,128)S(1)}, u32[]{:S(2)}) copy-start(f32[32,256,128]{2,1,0:T(8,128)S(1)} %convolution_add_fusion.1) | copy-start | bytes 12582916
  88.8 15.2 %copy-start.2 = (f32[32,256,128]{2,1,0:T(8,128)}, f32[32,256,128]{2,1,0:T(8,128)S(1)}, u32[]{:S(2)}) copy-start(f32[32,256,128]{2,1,0:T(8,128)S(1)} %convolution_subtract_fusion.1) | copy-start | bytes 12582916
  117.8 22.8 %copy-start.10 = (bf16[1024,512]{1,0:T(8,128)(2,1)S(1)}, bf16[1024,512]{1,0:T(8,128)(2,1)}, u32[]{:S(2)}) copy-start(bf16[1024,512]{1,0:T(8,128)(2,1)} %param.8) | copy-start | bytes 3145732
  117.8 22.8 %copy-start.11 = (bf16[1024,512]{1,0:T(8,128)(2,1)S(1)}, bf16[1024,512]{1,0:T(8,128)(2,1)}, u32[]{:S(2)}) copy-start(bf16[1024,512]{1,0:T(8,128)(2,1)} %param.9) | copy-start | bytes 3145732
  143.3 22.4 %all-to-all-start.1 = ((bf16[32,32,512]{2,1,0:T(8,128)(2,1)}), bf16[32,32,512]{2,1,0:T(8,128)(2,1)S(1)}, u32[]{:S(2)}, u32[]{:S(2)}) async-start(bf16[32,32,512]{2,1,0:T(8,128)(2,1)} %bitcast.11), calls=%async_computation.1 | async-start | bytes 2097152 | tf_op jit(solution)/shard_map/all_to_all | solution.py:132
  147.9 113.0 %all-gather.2.cloned.1.call-start = ((), (), s32[]{:S(2)}) async-start(), calls=%async_computation.7 | async-start | bytes 5242880 | tf_op jit(solution)/shard_map/all_gather | solution.py:103
  170.7 16.2 %copy-start.4 = (f32[32,128,256]{2,1,0:T(8,128)}, f32[32,128,256]{2,1,0:T(8,128)S(1)}, u32[]{:S(2)}) copy-start(f32[32,128,256]{2,1,0:T(8,128)S(1)} %fusion.80) | copy-start | bytes 12582916
  186.9 7.9 %copy-start.1 = (f32[32,256,128]{2,1,0:T(8,128)S(1)}, f32[32,256,128]{2,1,0:T(8,128)}, u32[]{:S(2)}) copy-start(f32[32,256,128]{2,1,0:T(8,128)} %copy-done) | copy-start | bytes 12582916
  187.0 7.9 %copy-start.3 = (f32[32,256,128]{2,1,0:T(8,128)S(1)}, f32[32,256,128]{2,1,0:T(8,128)}, u32[]{:S(2)}) copy-start(f32[32,256,128]{2,1,0:T(8,128)} %copy-done.2) | copy-start | bytes 12582916
  226.4 3.7 copy-start.8
  234.6 6.9 copy-start.12
  234.6 8.9 %copy-start.9 = (f32[256,256]{1,0:T(8,128)S(1)}, f32[256,256]{1,0:T(8,128)}, u32[]{:S(2)}) copy-start(f32[256,256]{1,0:T(8,128)} %copy-done.7) | copy-start | bytes 786436
  236.9 22.2 %all-to-all-start.2 = ((bf16[32,32,512]{2,0,1:T(8,128)(2,1)}), bf16[32,32,512]{2,0,1:T(8,128)(2,1)S(1)}, u32[]{:S(2)}, u32[]{:S(2)}) async-start(bf16[32,32,512]{2,0,1:T(8,128)(2,1)} %copy.107), calls=%async_computation.2 | async-start | bytes 2097152 | tf_op jit(solution)/shard_map/all_to_all | solution.py:135
  241.4 212.9 %reduce-scatter.7.cloned.1.call-start = ((), (), s32[]{:S(2)}) async-start(), calls=%async_computation.9 | async-start | bytes 8650752
  250.6 8.5 %copy-start.5 = (bf16[1024,512]{1,0:T(8,128)(2,1)S(1)}, bf16[1024,512]{1,0:T(8,128)(2,1)}, u32[]{:S(2)}) copy-start(bf16[1024,512]{1,0:T(8,128)(2,1)} %param.11) | copy-start | bytes 3145732
  250.6 8.5 %copy-start.6 = (bf16[1024,512]{1,0:T(8,128)(2,1)S(1)}, bf16[1024,512]{1,0:T(8,128)(2,1)}, u32[]{:S(2)}) copy-start(bf16[1024,512]{1,0:T(8,128)(2,1)} %param.7) | copy-start | bytes 3145732
  250.6 426.6 %reduce-scatter.5.cloned.1.call-start = ((), (), s32[]{:S(2)}) async-start(), calls=%async_computation.8 | async-start | bytes 17301504 | tf_op jit(solution)/shard_map/reduce_scatter | solution.py:104
Sparse Core Ops, SparseCore 0:
  150.4 47.6 all-gather.1
Sparse Core Ops, SparseCore 1:
  250.7 203.6 reduce-scatter.6
  456.6 220.5 reduce-scatter.4
